TPU v7x, 512 devices: a whole 4x4x16 slice. The times are simulated.
512 devices in a mesh: copy: 2 (over y_hi), dp: 32 (over z, y_lo), vocab: 8 (over x, core).
Axes of the slice: x: 4, y: 4 (y_hi: 2, y_lo: 2; y = y_hi * 2 + y_lo), z: 16, core: 2. Of those that a mesh axis runs over, the one named last changes fastest.
Arguments:
- hidden: bfloat16 [2, 768, 4096], P('copy', ('dp', 'vocab')), may hold values from -6 to 6
- head_weight: bfloat16 [2, 4096, 65536], P('copy', None, ('dp', 'vocab')), may hold values from -0.1875 to 0.1875
- targets: int32 [768], replicated, may hold values from 0 to 65535
Outputs:
- head_grad: bfloat16 [2, 4096, 65536], P('copy', None, ('dp', 'vocab'))
- loss_mean: float32 [2], P('copy')
All inputs are finite; a program needn't handle non-finite values.
Results may differ from a plain program's by a relative error of at most 0.0034.
Values may be sent and summed in bfloat16 or wider, within the bound.
A program may use at most 64 MiB of HBM per device.

v0:
```python
import jax
import jax.numpy as jnp
from jax import lax
from jax.sharding import Mesh
from jax.sharding import PartitionSpec as P

DP_VOCAB = ("dp_0", "dp_1", "vocab_0", "vocab_1")


distill_weight = 0.5


def piece_ends(length, count):
    hop = length // count
    if hop >= 8:
        hop -= hop % 8
    return [hop * k for k in range(1, count)]


def stacked_from(x, axes, order):
    parts = x
    for k in order:
        parts = lax.all_gather(parts, axes[k])
    done = order[::-1]
    back = [done.index(k) for k in range(len(axes))]
    parts = parts.transpose(*back, *range(len(axes), parts.ndim))
    return parts.reshape(-1, *x.shape)


def in_order(parts, dim):
    lengths = list(parts.shape[1:])
    lengths[dim] *= parts.shape[0]
    return jnp.moveaxis(parts, 0, dim).reshape(lengths)


def spread_gather(x, axes, dim):
    split_at = max(range(max(1, x.ndim - 1)), key=lambda d: x.shape[d])
    count, finished = (len(axes), [])
    for initial, share in enumerate(
        jnp.split(x, piece_ends(x.shape[split_at], count), axis=split_at)
    ):
        if share.size:
            order = [(initial - k) % count for k in range(count)]
            finished.append(stacked_from(share, axes, order))
    return in_order(jnp.concatenate(finished, axis=split_at + 1), dim)


def swapped(value, axis, distance):
    mask = 2**distance
    pairs = [(source, source ^ mask) for source in range(lax.axis_size(axis))]
    return lax.ppermute(value, axis, pairs)


def gathered_once(x, axis):
    leaves = jax.tree.leaves(x)
    order = sorted(range(len(leaves)), key=lambda k: -leaves[k].size)
    width = (1, *leaves[order[0]].shape)[-1]
    lines = [
        jnp.pad(leaves[k].reshape(-1), (0, -leaves[k].size % width)).reshape(-1, width)
        for k in order
    ]
    both, at, found = (lax.all_gather(jnp.concatenate(lines), axis), 0, {})
    for k, line in zip(order, lines):
        share = both[:, at : at + len(line)].reshape(len(both), -1)
        found[k] = share[:, : leaves[k].size].reshape(-1, *leaves[k].shape)
        at += len(line)
    numbers = iter(range(len(leaves)))
    return jax.tree.map(lambda _: found[next(numbers)], x)


def merged_by_axis(x, axes, combine):
    for axis in axes:
        pieces = gathered_once(x, axis)
        x = jax.tree.map(lambda part: part[0], pieces)
        for k in range(1, lax.axis_size(axis)):
            x = combine(x, jax.tree.map(lambda part: part[k], pieces))
    return x


def one_axis_at_a_time(x, axes):
    for axis in axes:
        x = lax.psum(x, axis)
    return x


def combine_stats(earlier, latter):
    result = []
    for position in range(0, len(earlier), 2):
        highest = jnp.maximum(earlier[position], latter[position])
        combined = earlier[position + 1] * jnp.exp(earlier[position] - highest) + latter[
            position + 1
        ] * jnp.exp(latter[position] - highest)
        result.append(highest)
        result.append(combined)
    return tuple(result)


def body(hidden, head_weight, targets):
    own_rows = hidden[0]
    weight = head_weight[0]
    columns_dev = weight.shape[1]
    offset = lax.axis_index(DP_VOCAB) * columns_dev
    total_rows = targets.shape[0]
    block_rows = total_rows // 4
    gathered = spread_gather(own_rows, DP_VOCAB, 0)
    logits = jnp.dot(gathered, weight, preferred_element_type=jnp.float32)
    partner_blocks = []
    for block in range(4):
        logit_block = logits[block * block_rows : (block + 1) * block_rows]
        partner_blocks.append(swapped(logit_block, "copy", 0))
    partner = jnp.concatenate(partner_blocks, axis=0)
    own_top = jnp.max(logits, axis=1)
    partner_top = jnp.max(partner, axis=1)
    own_sum = jnp.sum(jnp.exp(logits - own_top[:, None]), axis=1)
    partner_sum = jnp.sum(jnp.exp(partner - partner_top[:, None]), axis=1)
    own_top, own_sum, partner_top, partner_sum = merged_by_axis(
        (own_top, own_sum, partner_top, partner_sum), DP_VOCAB, combine_stats
    )
    own_lse = own_top + jnp.log(own_sum)
    partner_lse = partner_top + jnp.log(partner_sum)
    column_ids = offset + lax.broadcasted_iota(jnp.int32, (1, columns_dev), 1)
    onehot = (targets[:, None] == column_ids).astype(jnp.float32)
    own_probs = jnp.exp(logits - own_lse[:, None])
    partner_probs = jnp.exp(partner - partner_lse[:, None])
    grad_logits = (
        (1.0 + distill_weight) * own_probs - onehot - distill_weight * partner_probs
    ).astype(jnp.bfloat16)
    local_terms = jnp.sum(-onehot * logits + distill_weight * partner_probs * (partner - logits))
    loss_total = one_axis_at_a_time(local_terms, DP_VOCAB)
    row_terms = jnp.sum((1.0 + distill_weight) * own_lse - distill_weight * partner_lse)
    loss_mean = (row_terms + loss_total) / total_rows
    head_grad = lax.dot_general(
        gathered, grad_logits, (((0,), (0,)), ((), ())), preferred_element_type=jnp.float32
    )
    return (head_grad.astype(jnp.bfloat16)[None], loss_mean.reshape(1))


def solution(mesh):
    torus = Mesh(
        mesh.devices.reshape(mesh.shape["copy"], 16, 2, 4, 2),
        ("copy", "dp_0", "dp_1", "vocab_0", "vocab_1"),
    )
    in_specs = (P("copy", DP_VOCAB, None), P("copy", None, DP_VOCAB), P())
    out_specs = (P("copy", None, DP_VOCAB), P("copy"))
    return jax.shard_map(body, mesh=torus, in_specs=in_specs, out_specs=out_specs, check_vma=False)
```

profile of v0, /device:TPU:1, one launch (start us, length us, event | category | flops | bytes accessed | tf_op | source)
XLA Modules:
  0.0 297.0 jit_solution(13716197854560249258)
XLA Ops:
  7.2 8.7 %all_gather.45 = bf16[2,3,4096]{2,1,0:T(4,128)(2,1)S(1)} all-gather(bf16[1,3,4096]{2,1,0:T(4,128)(2,1)} %param.3), channel_id=1, replica_groups=mesh['copy'=2,'dp_0'=16,'dp_1'=2,'vocab_0'=4,'vocab_1'=2] {'vocab_1'}, dimensions={0}, use_global_device_ids=true | all-gather | bytes 73728 | tf_op jit(solution)/shard_map/all_gather | solution.py:23
  16.0 9.4 %all-gather = bf16[8,3,4096]{2,1,0:T(4,128)(2,1)S(1)} all-gather(bf16[2,3,4096]{2,1,0:T(4,128)(2,1)S(1)} %all_gather.45), channel_id=2, replica_groups=mesh['copy'=2,'dp_0'=16,'dp_1'=2,'vocab_0'=4,'vocab_1'=2] {'vocab_0'}, dimensions={0}, use_global_device_ids=true | all-gather | bytes 245760 | tf_op jit(solution)/shard_map/all_gather | solution.py:23
  25.3 0.2 copy.7
  25.6 5.2 %all-gather.1 = bf16[8,2,3,4096]{3,1,2,0:T(2,128)(2,1)S(1)} all-gather(bf16[4,2,3,4096]{3,1,2,0:T(2,128)(2,1)S(1)} %copy.7), channel_id=3, replica_groups=mesh['copy'=2,'dp_0'=16,'dp_1'=2,'vocab_0'=4,'vocab_1'=2] {'dp_1'}, dimensions={0}, use_global_device_ids=true | all-gather | bytes 589824 | tf_op jit(solution)/shard_map/all_gather | solution.py:23
  30.8 1.1 copy.8
  31.8 87.1 %all-gather.13.cloned.1.call-done = bf16[32,4,2,3,4096]{4,1,3,2,0:T(4,128)(2,1)} async-done(((bf16[2,4,2,3,4096]{4,1,3,2,0:T(4,128)(2,1)}), bf16[32,4,2,3,4096]{4,1,3,2,0:T(4,128)(2,1)}) %all-gather.13.cloned.1.call-update) | async-done | bytes 6291472 | tf_op jit(solution)/shard_map/all_gather | solution.py:23
  118.9 15.6 %copy.9 = bf16[32,4,2,3,4096]{4,3,2,1,0:T(4,128)(2,1)} copy(bf16[32,4,2,3,4096]{4,1,3,2,0:T(4,128)(2,1)} %all-gather.13.cloned.1.call-done) | data formatting | bytes 12582912 | tf_op jit(solution)/shard_map/all_gather | solution.py:23
  134.5 13.7 %reshape_reshape.3 = bf16[768,4096]{1,0:T(8,128)(2,1)} reshape(bf16[32,4,2,3,4096]{4,3,2,1,0:T(4,128)(2,1)} %copy.9) | data formatting | bytes 12582912 | tf_op jit(solution)/shard_map/reshape;reshape | solution.py:33
  148.2 4.7 %fusion.180 = (f32[768]{0:T(1024)S(1)}, f32[768,256]{1,0:T(8,128)S(1)}) fusion(bf16[768,4096]{1,0:T(8,128)(2,1)} %reshape_reshape.3, bf16[1,4096,256]{2,1,0:T(8,128)(2,1)S(1)} %copy-done), kind=kOutput, calls=%fused_computation.289 | convolution fusion | flops 1610808576 | bytes 9178112 | tf_op jit(solution)/shard_map/dot_general | solution.py:106
  153.0 4.4 %collective-permute-start = (f32[192,256]{1,0:T(8,128)S(1)}, f32[192,256]{1,0:T(8,128)S(1)}, u32[]{:S(2)}, u32[]{:S(2)}) collective-permute-start(f32[192,256]{1,0:T(8,128)S(1)} %get-tuple-element.34), channel_id=1, source_target_pairs={{0,256},{256,0},{1,257},{257,1},{2,258},{258,2},{3,259},{259,3},{4... | collective-permute-start | bytes 589832 | tf_op jit(solution)/shard_map/ppermute | solution.py:51
  157.4 2.4 collective-permute-start.1
  159.8 4.4 %collective-permute-start.2 = (f32[192,256]{1,0:T(8,128)S(1)}, f32[192,256]{1,0:T(8,128)S(1)}, u32[]{:S(2)}, u32[]{:S(2)}) collective-permute-start(f32[192,256]{1,0:T(8,128)S(1)} %get-tuple-element.32), channel_id=1, source_target_pairs={{0,256},{256,0},{1,257},{257,1},{2,258},{258,2},{3,259},{259,3},{4... | collective-permute-start | bytes 589832 | tf_op jit(solution)/shard_map/ppermute | solution.py:51
  164.2 2.4 collective-permute-start.3
  166.6 0.3 exponential_reduce_fusion.1
  167.0 2.7 collective-permute-done.2
  169.8 4.8 %collective-permute-done.3 = f32[192,256]{1,0:T(8,128)S(1)} collective-permute-done((f32[192,256]{1,0:T(8,128)S(1)}, f32[192,256]{1,0:T(8,128)S(1)}, u32[]{:S(2)}, u32[]{:S(2)}) %collective-permute-start.3) | collective-permute-done | bytes 196640 | tf_op jit(solution)/shard_map/ppermute | solution.py:51
  174.6 0.2 reduce_max.19
  174.8 0.3 exponential_reduce_fusion
  175.1 22.8 %all-gather.7 = f32[16,4,768]{2,1,0:T(4,128)S(1)} all-gather(f32[1,4,768]{2,1,0:T(4,128)S(1)} %maximum_bitcast_fusion), channel_id=5, replica_groups=mesh['copy'=2,'dp_0'=16,'dp_1'=2,'vocab_0'=4,'vocab_1'=2] {'dp_0'}, dimensions={0}, use_global_device_ids=true | all-gather | bytes 208896 | tf_op jit(solution)/shard_map/all_gather | solution.py:62
  198.0 0.2 fusion.89
  198.1 0.2 fusion.44
  198.3 3.2 %all-gather.8 = f32[2,4,768]{2,1,0:T(4,128)S(1)} all-gather(f32[1,4,768]{2,1,0:T(4,128)S(1)} %maximum_bitcast_fusion.1), channel_id=6, replica_groups=mesh['copy'=2,'dp_0'=16,'dp_1'=2,'vocab_0'=4,'vocab_1'=2] {'dp_1'}, dimensions={0}, use_global_device_ids=true | all-gather | bytes 36864 | tf_op jit(solution)/shard_map/all_gather | solution.py:62
  201.7 9.3 %all-gather.9 = f32[4,4,768]{2,1,0:T(4,128)S(1)} all-gather(f32[1,4,768]{2,1,0:T(4,128)S(1)} %maximum_bitcast_fusion.2), channel_id=7, replica_groups=mesh['copy'=2,'dp_0'=16,'dp_1'=2,'vocab_0'=4,'vocab_1'=2] {'vocab_0'}, dimensions={0}, use_global_device_ids=true | all-gather | bytes 61440 | tf_op jit(solution)/shard_map/all_gather | solution.py:62
  211.1 14.2 %all-gather.10 = f32[2,4,768]{2,1,0:T(4,128)S(1)} all-gather(f32[1,4,768]{2,1,0:T(4,128)S(1)} %maximum_bitcast_fusion.3), channel_id=8, replica_groups=mesh['copy'=2,'dp_0'=16,'dp_1'=2,'vocab_0'=4,'vocab_1'=2] {'vocab_1'}, dimensions={0}, use_global_device_ids=true | all-gather | bytes 36864 | tf_op jit(solution)/shard_map/all_gather | solution.py:62
  225.4 0.6 subtract_reduce_fusion
  226.0 2.2 fusion.7
  228.2 22.1 %psum.28 = f32[]{:T(128)} all-reduce(f32[]{:T(128)} %fusion.7), channel_id=1, replica_groups=mesh['copy'=2,'dp_0'=16,'dp_1'=2,'vocab_0'=4,'vocab_1'=2] {'dp_0'}, use_global_device_ids=true, to_apply=%region_6.7 | all-reduce | flops 1 | bytes 8 | tf_op jit(solution)/shard_map/psum | solution.py:82
  250.4 4.6 %psum.29 = f32[]{:T(128)} all-reduce(f32[]{:T(128)} %psum.28), channel_id=1, replica_groups=mesh['copy'=2,'dp_0'=16,'dp_1'=2,'vocab_0'=4,'vocab_1'=2] {'dp_1'}, use_global_device_ids=true, to_apply=%region_7.8 | all-reduce | flops 1 | bytes 8 | tf_op jit(solution)/shard_map/psum | solution.py:82
  254.9 8.7 %psum.30 = f32[]{:T(128)} all-reduce(f32[]{:T(128)} %psum.29), channel_id=1, replica_groups=mesh['copy'=2,'dp_0'=16,'dp_1'=2,'vocab_0'=4,'vocab_1'=2] {'vocab_0'}, use_global_device_ids=true, to_apply=%region_8.9 | all-reduce | flops 1 | bytes 8 | tf_op jit(solution)/shard_map/psum | solution.py:82
  263.6 13.5 %psum.31 = f32[]{:T(128)} all-reduce(f32[]{:T(128)} %psum.30), channel_id=1, replica_groups=mesh['copy'=2,'dp_0'=16,'dp_1'=2,'vocab_0'=4,'vocab_1'=2] {'vocab_1'}, use_global_device_ids=true, to_apply=%region_9.10 | all-reduce | flops 1 | bytes 8 | tf_op jit(solution)/shard_map/psum | solution.py:82
  277.1 6.5 %fusion = bf16[1,4096,256]{1,2,0:T(8,128)(2,1)} fusion(bf16[768,4096]{1,0:T(8,128)(2,1)} %reshape_reshape.3, f32[768,256]{1,0:T(8,128)S(1)} %constant_dynamic-update-slice_fusion, f32[768,256]{1,0:T(8,128)} %copy-done.1, f32[768]{0:T(1024)S(1)} %get-tuple-element.18, s32[256]{0:T(256)S(1)} %iota_add_fusion, f32[768]{0:T(1024)S(1)} %get-tuple-element.17, ...), kind=kOutput, calls=%fused_computation.1 | convolution fusion | flops 1613430784 | bytes 9971712 | tf_op jit(solution)/shard_map/dot_general | solution.py:132
  283.7 4.1 %copy.10 = bf16[1,4096,256]{2,1,0:T(8,128)(2,1)} copy(bf16[1,4096,256]{1,2,0:T(8,128)(2,1)} %fusion) | data formatting | bytes 4194304
  (27 shorter events, 0.5 us)
Async XLA Ops:
  7.2 141.1 %copy-start = (bf16[1,4096,256]{2,1,0:T(8,128)(2,1)S(1)}, bf16[1,4096,256]{2,1,0:T(8,128)(2,1)}, u32[]{:S(2)}) copy-start(bf16[1,4096,256]{2,1,0:T(8,128)(2,1)} %param.4) | copy-start | bytes 6291460
  7.2 111.7 %all-gather.13.cloned.1.call-start = ((), (), s32[]{:S(2)}) async-start(), calls=%async_computation | async-start | bytes 6684672 | tf_op jit(solution)/shard_map/all_gather | solution.py:23
  148.2 77.8 %copy-start.2 = (s32[768]{0:T(1024)S(1)}, s32[768]{0:T(1024)}, u32[]{:S(2)}) copy-start(s32[768]{0:T(1024)} %param.5) | copy-start | bytes 9220
  152.9 16.8 %copy-start.1 = (f32[768,256]{1,0:T(8,128)}, f32[768,256]{1,0:T(8,128)S(1)}, u32[]{:S(2)}) copy-start(f32[768,256]{1,0:T(8,128)S(1)} %get-tuple-element.40) | copy-start | bytes 2359300
  153.0 13.9 %collective-permute-start = (f32[192,256]{1,0:T(8,128)S(1)}, f32[192,256]{1,0:T(8,128)S(1)}, u32[]{:S(2)}, u32[]{:S(2)}) collective-permute-start(f32[192,256]{1,0:T(8,128)S(1)} %get-tuple-element.34), channel_id=1, source_target_pairs={{0,256},{256,0},{1,257},{257,1},{2,258},{258,2},{3,259},{259,3},{4... | collective-permute-start | bytes 589832 | tf_op jit(solution)/shard_map/ppermute | solution.py:51
  157.4 9.6 %collective-permute-start.1 = (f32[192,256]{1,0:T(8,128)S(1)}, f32[192,256]{1,0:T(8,128)S(1)}, u32[]{:S(2)}, u32[]{:S(2)}) collective-permute-start(f32[192,256]{1,0:T(8,128)S(1)} %get-tuple-element.33), channel_id=1, source_target_pairs={{0,256},{256,0},{1,257},{257,1},{2,258},{258,2},{3,259},{259,3},{4... | collective-permute-start | bytes 589832 | tf_op jit(solution)/shard_map/ppermute | solution.py:51
  159.8 9.9 %collective-permute-start.2 = (f32[192,256]{1,0:T(8,128)S(1)}, f32[192,256]{1,0:T(8,128)S(1)}, u32[]{:S(2)}, u32[]{:S(2)}) collective-permute-start(f32[192,256]{1,0:T(8,128)S(1)} %get-tuple-element.32), channel_id=1, source_target_pairs={{0,256},{256,0},{1,257},{257,1},{2,258},{258,2},{3,259},{259,3},{4... | collective-permute-start | bytes 589832 | tf_op jit(solution)/shard_map/ppermute | solution.py:51
  164.2 10.4 %collective-permute-start.3 = (f32[192,256]{1,0:T(8,128)S(1)}, f32[192,256]{1,0:T(8,128)S(1)}, u32[]{:S(2)}, u32[]{:S(2)}) collective-permute-start(f32[192,256]{1,0:T(8,128)S(1)} %get-tuple-element.31), channel_id=1, source_target_pairs={{0,256},{256,0},{1,257},{257,1},{2,258},{258,2},{3,259},{259,3},{4... | collective-permute-start | bytes 589832 | tf_op jit(solution)/shard_map/ppermute | solution.py:51
Sparse Core Ops, SparseCore 0:
  31.9 86.9 all-gather.12
where the time goes:
time: 298 us; the launch traced here: 297 us
  blocking collectives  122 us (41%)
  waiting for transfers between devices  94.7 us (32%)
  local copies, waits for them, and re-layouts  34.9 us (12%)
  between operations  16.6 us (6%)
  starting transfers between devices  13.6 us (5%)
  matrix products  11.2 us (4%)
  other arithmetic  4.13 us (1%)
    all_gather x1, waiting for transfers between devices, stacked_from(): parts = lax.all_gather(parts, axes[k])  87.1 us
    all_gather x4, blocking collectives, gathered_once(): both, at, found = (lax.all_gather(jnp.concatenate(lines), axis), 0, {})  49.7 us
    psum x4, blocking collectives, one_axis_at_a_time(): x = lax.psum(x, axis)  48.9 us
    all_gather x3, blocking collectives, stacked_from(): parts = lax.all_gather(parts, axes[k])  23.3 us
    all_gather x3, local copies, waits for them, and re-layouts, stacked_from(): parts = lax.all_gather(parts, axes[k])  16.9 us
    another operation x1, local copies, waits for them, and re-layouts, in_order(): return jnp.moveaxis(parts, 0, dim).reshape(lengths)  13.7 us
    ppermute x4, starting transfers between devices, swapped(): return lax.ppermute(value, axis, pairs)  13.6 us
    ppermute x4, waiting for transfers between devices, swapped(): return lax.ppermute(value, axis, pairs)  7.57 us
  transfers between devices with their start and end apart: 5, of which 3 were waited for; matrix products, arithmetic and copies ran while one was open for 0% of the time, Pallas kernels for 0%

commit v1 on v0

v1 whole, which is shorter than its diff:
```python
import functools

import jax
import jax.numpy as jnp
from jax import lax
from jax.experimental import pallas as pl
from jax.experimental.pallas import tpu as pltpu
from jax.sharding import Mesh
from jax.sharding import PartitionSpec as P

Z, Y, X, C = 16, 2, 4, 2
PEERS = Y * X * C
D = 4096
COLS = 256
ROWS = 3
PLANE = PEERS * ROWS
TOKENS = Z * PLANE
UNIT = D // PEERS
HALF = PEERS // 2
CHUNKS = 4
STEPS = Z // 2
LAG = 4
LANES = 128
GROUPS = TOKENS // LANES
TINY = 1e-37
DISTILL = 0.5

MESH = pl.DeviceIdType.MESH
F32 = jnp.float32
BF16 = jnp.bfloat16


def arrived(ref, sem):
    pltpu.make_async_copy(ref, ref, sem).wait()


def send(src, dst, send_sem, recv_sem, **where):
    pltpu.make_async_remote_copy(
        src_ref=src,
        dst_ref=dst,
        send_sem=send_sem,
        recv_sem=recv_sem,
        device_id=where,
        device_id_type=MESH,
    ).start()


def plane_peer(j):
    return {"y": j // (X * C), "x": lax.rem(j // C, X), "c": lax.rem(j, C)}


def kernel(
    hidden_ref, targets_ref, weight_hbm, grad_hbm, loss_ref,
    hbuf, weight, pad, abuf, logits, ebuf, pbuf, mcol, lcol,
    srow, s1, s2, prow, rrow, rbuf, lossv, lrow, l1, l2, obuf,
    wsem, osem, asem, zsem_a, zsem_b, bsem, ysem, xsem, qsem, csem, esem, ssem, rsem, out_sems,
):
    z, y, x, c = (lax.axis_index(n) for n in ("z", "y", "x", "c"))
    copy = lax.axis_index("copy")
    me = (y * X + x) * C + c
    unit = c * HALF + x * Y + y

    load_weight = pltpu.make_async_copy(weight_hbm, weight, wsem)
    load_weight.start()

    barrier = pltpu.get_barrier_semaphore()

    def greet(k, carry):
        pl.semaphore_signal(
            barrier, inc=1, device_id=plane_peer(lax.rem(me + k, PEERS)), device_id_type=MESH
        )
        pl.semaphore_signal(
            barrier, inc=1, device_id={"z": lax.rem(z + k, Z)}, device_id_type=MESH
        )
        return carry

    lax.fori_loop(1, PEERS, greet, 0)
    pl.semaphore_signal(barrier, inc=1, device_id={"copy": 1 - copy}, device_id_type=MESH)

    own = hidden_ref[0].astype(F32)
    pad[...] = jnp.zeros_like(pad)
    for q in range(PEERS):
        pad[q, 0:ROWS, :] = own[:, q * UNIT : (q + 1) * UNIT]

    pl.semaphore_wait(barrier, 2 * (PEERS - 1) + 1)

    def unit_of(j):
        return lax.rem(j, C) * HALF + lax.rem(j // C, X) * Y + j // (X * C)

    def scatter(k, carry):
        j = lax.rem(me + k, PEERS)
        send(pad.at[unit_of(j)], abuf.at[me], out_sems.at[0], asem, **plane_peer(j))
        return carry

    lax.fori_loop(1, PEERS, scatter, 0)
    abuf[pl.ds(me, 1)] = pad[pl.ds(unit, 1)]
    arrived(abuf.at[pl.ds(0, PEERS - 1)], asem)

    row = lax.broadcasted_iota(jnp.int32, (PLANE, PEERS * 8), 0)
    col = lax.broadcasted_iota(jnp.int32, (PLANE, PEERS * 8), 1)
    pick = (row == ROWS * (col >> 3) + (col & 7)) & ((col & 7) < ROWS)
    block = abuf[...].reshape(PEERS * 8, UNIT).astype(BF16)
    packed = jnp.dot(jnp.where(pick, 1.0, 0.0).astype(BF16), block, preferred_element_type=F32)
    hbuf[z, unit] = packed.astype(BF16)

    def at(p, first, count):
        return hbuf.at[p, pl.ds(first, count)]

    def back(t):
        return lax.rem(z - t + Z, Z)

    def ahead(t):
        return lax.rem(z + t, Z)

    right, left = ahead(1), back(1)

    def move(ref, sem_out, sem_in, **where):
        send(ref, ref, out_sems.at[sem_out], sem_in, **where)

    def a_enter(p, t, direction):
        ref = at(p, unit, 1)

        @pl.when(t > 0)
        def _():
            arrived(ref, zsem_a.at[direction, t])

        @pl.when(t < STEPS - direction)
        def _():
            move(ref, 1, zsem_a.at[direction, t + 1], z=right if direction == 0 else left)

    def a_first(p):
        move(at(p, unit, 1), 2, ysem.at[p], y=1 - y)

    def a_second(p):
        arrived(at(p, unit, 1), ysem.at[p])
        ref = at(p, x * Y, Y)
        move(ref, 3, xsem.at[0, p], x=lax.rem(x + 1, X))
        move(ref, 3, xsem.at[1, p], x=lax.rem(x + X - 1, X))
        move(ref, 4, csem.at[p], c=1 - c)

    def a_third(p):
        lower, upper = lax.rem(x + X - 1, X), lax.rem(x + 1, X)
        ref = at(p, lower * Y, Y)
        arrived(ref, xsem.at[0, p])
        move(at(p, lower * Y, 1), 5, qsem.at[p], x=upper)
        move(ref, 4, csem.at[p], c=1 - c)
        ref = at(p, upper * Y, Y)
        arrived(ref, xsem.at[1, p])
        move(at(p, upper * Y + 1, 1), 5, qsem.at[p], x=lower)
        move(ref, 4, csem.at[p], c=1 - c)

    def a_fourth(p):
        ref = at(p, lax.rem(x + 2, X) * Y, Y)
        arrived(ref, qsem.at[p])
        move(ref, 4, csem.at[p], c=1 - c)

    def for_planes(t, first, do):
        @pl.when((t >= first) & (t <= STEPS))
        def _():
            do(back(t))

        @pl.when((t >= 1) & (t <= STEPS - 1))
        def _():
            do(ahead(t))

    def b_spread(k, carry):
        j = lax.rem(me // C + k, HALF)
        move(at(z, unit, 1), 6, bsem, y=j // X, x=lax.rem(j, X))
        return carry

    def b_enter(p, t, direction):
        for k in range(CHUNKS):
            size = HALF // CHUNKS
            ref = at(p, HALF + k * size, size)

            @pl.when(t > 0)
            def _():
                arrived(ref, zsem_b.at[direction, t, k])

            @pl.when(t < STEPS - direction)
            def _():
                move(ref, 7, zsem_b.at[direction, t + 1, k], z=right if direction == 0 else left)

            if direction == 0:
                move(ref, 4, csem.at[p], c=1 - c)
            else:
                @pl.when(t > 0)
                def _():
                    move(ref, 4, csem.at[p], c=1 - c)

    @pl.when(c == 1)
    def _():
        lax.fori_loop(1, HALF, b_spread, 0)
        arrived(hbuf.at[z, pl.ds(HALF, HALF - 1)], bsem)

    load_weight.wait()

    def compute(u):
        planes = (back(u), ahead(u - 1))
        for p in planes:
            arrived(at(p, (1 - c) * HALF, HALF), csem.at[p])
        acc = jnp.zeros((2 * PLANE, COLS), F32)
        for q in range(PEERS):
            both = jnp.concatenate([hbuf[p, q] for p in planes], axis=0)
            acc += jnp.dot(both, weight[q * UNIT : (q + 1) * UNIT, :], preferred_element_type=F32)
        top = jnp.max(acc, axis=1, keepdims=True)
        e = jnp.exp(acc - top)
        lse = top + jnp.log(jnp.sum(e, axis=1, keepdims=True))
        for k, p in enumerate(planes):
            own_rows = slice(k * PLANE, (k + 1) * PLANE)
            rows = pl.ds(pl.multiple_of(p * PLANE, PLANE), PLANE)
            logits[rows, :] = acc[own_rows]
            mcol[rows, :] = top[own_rows]
            lcol[rows, :] = lse[own_rows]
            ebuf[rows, :] = e[own_rows].astype(BF16)
            send(
                ebuf.at[rows, :], pbuf.at[rows, :], out_sems.at[8], esem, copy=1 - copy
            )

    def step(i, carry):
        @pl.when(c == 0)
        def _():
            @pl.when(i <= STEPS)
            def _():
                a_enter(back(i), i, 0)

            @pl.when(i <= STEPS - 1)
            def _():
                a_enter(ahead(i), i, 1)

            for_planes(i, 0, a_first)
            for_planes(i - 1, 0, a_second)
            for_planes(i - 2, 0, a_third)
            for_planes(i - 3, 0, a_fourth)

        @pl.when(c == 1)
        def _():
            @pl.when(i <= STEPS)
            def _():
                b_enter(back(i), i, 0)

            @pl.when(i <= STEPS - 1)
            def _():
                b_enter(ahead(i), i, 1)

        @pl.when(i > LAG)
        def _():
            compute(i - LAG)

        return carry

    lax.fori_loop(0, STEPS + LAG + 1, step, 0)

    eye = lax.broadcasted_iota(jnp.int32, (LANES, LANES), 0) == lax.broadcasted_iota(
        jnp.int32, (LANES, LANES), 1
    )

    def to_row(column):
        return jnp.sum(jnp.where(eye, column, 0.0), axis=0, keepdims=True)

    def to_column(row):
        return jnp.sum(jnp.where(eye, row, 0.0), axis=1, keepdims=True)

    srow[...] = jnp.zeros_like(srow)
    for b in range(GROUPS):
        rows = slice(b * LANES, (b + 1) * LANES)
        srow[b : b + 1, :] = to_row(lcol[rows, :])

    def to_plane(src, dst, sem_out, sem_in):
        def one(k, carry):
            send(src, dst.at[me], out_sems.at[sem_out], sem_in, **plane_peer(lax.rem(me + k, PEERS)))
            return carry

        lax.fori_loop(1, PEERS, one, 0)
        dst[pl.ds(me, 1)] = src[...][None]

    def to_line(src, dst, sem_out, sem_in):
        def one(k, carry):
            send(src, dst.at[z], out_sems.at[sem_out], sem_in, z=lax.rem(z + k, Z))
            return carry

        lax.fori_loop(1, Z, one, 0)
        dst[pl.ds(z, 1)] = src[...][None]

    def merged(parts):
        top = jnp.max(parts, axis=0)
        return top + jnp.log(jnp.sum(jnp.exp(parts - top[None]), axis=0))

    to_plane(srow, s1, 9, ssem.at[0])
    arrived(s1.at[pl.ds(0, PEERS - 1)], ssem.at[0])
    prow[...] = merged(s1[...])
    to_line(prow, s2, 10, ssem.at[1])
    arrived(s2.at[pl.ds(0, Z - 1)], ssem.at[1])
    total = merged(s2[...])

    rrow[...] = jnp.zeros_like(rrow)
    for b in range(GROUPS):
        rows = slice(b * LANES, (b + 1) * LANES)
        rrow[b : b + 1, :] = to_row(mcol[rows, :]) - total[b : b + 1, :]
    send(rrow, rbuf, out_sems.at[11], rsem, copy=1 - copy)
    arrived(rbuf, rsem)
    arrived(pbuf, esem)

    offset = ((z * Y + y) * (X * C) + x * C + c) * COLS
    ids = offset + lax.broadcasted_iota(jnp.int32, (LANES, COLS), 1)
    loss = jnp.zeros((8, COLS), F32)
    grads = []
    for b in range(GROUPS):
        rows = slice(b * LANES, (b + 1) * LANES)
        log_p = logits[rows, :] - to_column(total[b : b + 1, :])
        log_scale = to_column(rbuf[b : b + 1, :])
        other = pbuf[rows, :].astype(F32)
        log_o = jnp.log(jnp.maximum(other, TINY)) + log_scale
        other = other * jnp.exp(log_scale)
        target = to_column(targets_ref[b : b + 1, :].astype(F32)).astype(jnp.int32)
        hot = jnp.where(ids == target, 1.0, 0.0)
        grads.append(((1.0 + DISTILL) * jnp.exp(log_p) - hot - DISTILL * other).astype(BF16).T)
        terms = DISTILL * other * (log_o - log_p) - hot * log_p
        loss += jnp.sum(terms.reshape(LANES // 8, 8, COLS), axis=0)
    grads = jnp.concatenate(grads, axis=1)
    lossv[...] = loss[:, :LANES] + loss[:, LANES:]
    to_plane(lossv, l1, 12, ssem.at[2])

    def grad_piece(q):
        block = hbuf[:, q].reshape(TOKENS, UNIT)
        flipped = jnp.dot(grads, block, preferred_element_type=F32)
        obuf[q] = flipped.astype(BF16).T
        pltpu.make_async_copy(obuf.at[q], grad_hbm.at[pl.ds(q * UNIT, UNIT), :], osem).start()

    for q in range(HALF):
        grad_piece(q)
    arrived(l1.at[pl.ds(0, PEERS - 1)], ssem.at[2])
    lrow[...] = jnp.sum(l1[...], axis=0)
    for q in range(HALF, PEERS):
        grad_piece(q)
    to_line(lrow, l2, 13, ssem.at[3])
    arrived(l2.at[pl.ds(0, Z - 1)], ssem.at[3])
    loss_ref[0] = jnp.sum(l2[...]) * (1.0 / TOKENS)

    units = hbuf.at[0]
    arrived(pad.at[pl.ds(0, PEERS - 1)], out_sems.at[0])
    arrived(hbuf.at[pl.ds(0, HALF)], out_sems.at[4])

    @pl.when(c == 0)
    def _():
        arrived(units.at[pl.ds(0, Z - 1)], out_sems.at[1])
        arrived(units, out_sems.at[2])
        arrived(hbuf.at[pl.ds(0, 4)], out_sems.at[3])
        arrived(hbuf.at[pl.ds(0, 2)], out_sems.at[5])

    @pl.when(c == 1)
    def _():
        arrived(units.at[pl.ds(0, HALF - 1)], out_sems.at[6])
        arrived(hbuf.at[pl.ds(0, Z - 1), pl.ds(0, HALF)], out_sems.at[7])

    arrived(ebuf, out_sems.at[8])
    arrived(s1.at[pl.ds(0, PEERS - 1)], out_sems.at[9])
    arrived(s1.at[pl.ds(0, Z - 1)], out_sems.at[10])
    arrived(rrow, out_sems.at[11])
    arrived(s1.at[pl.ds(0, PEERS - 1)], out_sems.at[12])
    arrived(s1.at[pl.ds(0, Z - 1)], out_sems.at[13])
    arrived(obuf, osem)


def body(hidden, head_weight, targets):
    dma = pltpu.SemaphoreType.DMA
    stat = (8, LANES)
    grad, loss = pl.pallas_call(
        kernel,
        out_shape=(
            jax.ShapeDtypeStruct((D, COLS), BF16),
            jax.ShapeDtypeStruct((1,), F32),
        ),
        in_specs=[
            pl.BlockSpec(memory_space=pltpu.VMEM),
            pl.BlockSpec(memory_space=pltpu.VMEM),
            pl.BlockSpec(memory_space=pl.ANY),
        ],
        out_specs=(
            pl.BlockSpec(memory_space=pl.ANY),
            pl.BlockSpec(memory_space=pltpu.SMEM),
        ),
        scratch_shapes=[
            pltpu.VMEM((Z, PEERS, PLANE, UNIT), BF16),
            pltpu.VMEM((D, COLS), BF16),
            pltpu.VMEM((PEERS, 8, UNIT), F32),
            pltpu.VMEM((PEERS, 8, UNIT), F32),
            pltpu.VMEM((TOKENS, COLS), F32),
            pltpu.VMEM((TOKENS, COLS), BF16),
            pltpu.VMEM((TOKENS, COLS), BF16),
            pltpu.VMEM((TOKENS, 1), F32),
            pltpu.VMEM((TOKENS, 1), F32),
            pltpu.VMEM(stat, F32),
            pltpu.VMEM((PEERS, *stat), F32),
            pltpu.VMEM((Z, *stat), F32),
            pltpu.VMEM(stat, F32),
            pltpu.VMEM(stat, F32),
            pltpu.VMEM(stat, F32),
            pltpu.VMEM(stat, F32),
            pltpu.VMEM(stat, F32),
            pltpu.VMEM((PEERS, *stat), F32),
            pltpu.VMEM((Z, *stat), F32),
            pltpu.VMEM((PEERS, UNIT, COLS), BF16),
            dma,
            dma,
            dma,
            dma((2, STEPS + 1)),
            dma((2, STEPS + 1, CHUNKS)),
            dma,
            dma((Z,)),
            dma((2, Z)),
            dma((Z,)),
            dma((Z,)),
            dma,
            dma((4,)),
            dma,
            dma((14,)),
        ],
        compiler_params=pltpu.CompilerParams(
            collective_id=0, has_side_effects=True, vmem_limit_bytes=48 * 1024 * 1024
        ),
        cost_estimate=pl.CostEstimate(
            flops=4 * TOKENS * D * COLS,
            bytes_accessed=4 * D * COLS,
            transcendentals=3 * TOKENS * COLS,
        ),
    )(hidden, targets.reshape(GROUPS, LANES), head_weight[0])
    return grad[None], loss


def solution(mesh):
    torus = Mesh(
        mesh.devices.reshape(mesh.shape["copy"], Z, Y, X, C), ("copy", "z", "y", "x", "c")
    )
    everywhere = ("z", "y", "x", "c")
    in_specs = (P("copy", everywhere, None), P("copy", None, everywhere), P())
    out_specs = (P("copy", None, everywhere), P("copy"))
    return jax.shard_map(body, mesh=torus, in_specs=in_specs, out_specs=out_specs, check_vma=False)
```

time: 298 us -> 101 us (0.34)
  blocking collectives: 122 us -> 0 us
  waiting for transfers between devices: 94.7 us -> 0 us
  Pallas kernels: 0 us -> 93.5 us
  local copies, waits for them, and re-layouts: 34.9 us -> 4.35 us
  between operations: 16.6 us -> 2.39 us
  starting transfers between devices: 13.6 us -> 0 us
  matrix products: 11.2 us -> 0 us
  other arithmetic: 4.13 us -> 0 us
    pallas_call x0 -> x1, Pallas kernels: none -> 93.5 us  [body(): pl.pallas_call(kernel, out_shape=(jax.ShapeDtypeStruct((D, COLS), BF16),...]
    all_gather x1 -> x0, waiting for transfers between devices: 87.1 us -> none  [stacked_from(): parts = lax.all_gather(parts, axes[k])]
    all_gather x7 -> x0, blocking collectives: 72.9 us -> none  [the longest x4 49.7 us: gathered_once(): both, at, found = (lax.all_gather(jnp.concatenate(lines), axis), 0, {})]
    psum x4 -> x0, blocking collectives: 48.9 us -> none  [one_axis_at_a_time(): x = lax.psum(x, axis)]
    all_gather x3 -> x0, local copies, waits for them, and re-layouts: 16.9 us -> none  [stacked_from(): parts = lax.all_gather(parts, axes[k])]
    another operation x1 -> x0, local copies, waits for them, and re-layouts: 13.7 us -> none  [in_order(): return jnp.moveaxis(parts, 0, dim).reshape(lengths)]
    ppermute x4 -> x0, starting transfers between devices: 13.6 us -> none  [swapped(): return lax.ppermute(value, axis, pairs)]
    dot_general x2 -> x0, matrix products: 11.2 us -> none  [the longest x1 6.54 us: body(): lax.dot_general(gathered, grad_logits, (((0,), (0,)), ((), ())), preferre...]
  transfers between devices with their start and end apart: 5 -> 0, of which waited for: 3 -> 0; matrix products, arithmetic and copies ran while one was open for 0% -> 0% of each run, Pallas kernels for 0% -> 0%
where the time goes in v1:
time: 101 us; the launch traced here: 100 us
  Pallas kernels  93.5 us (93%)
  local copies, waits for them, and re-layouts  4.35 us (4%)
  between operations  2.39 us (2%)
    pallas_call x1, Pallas kernels, body(): pl.pallas_call(kernel, out_shape=(jax.ShapeDtypeStruct((D, COLS), BF16),...  93.5 us
    unnamed x7, local copies, waits for them, and re-layouts  4.35 us

profile of v1, /device:TPU:1, one launch (start us, length us, event | category | flops | bytes accessed | tf_op | source)
XLA Modules:
  0.0 100.2 jit_solution(3408640618887342057)
XLA Ops:
  0.6 0.0 copy-start
  0.6 1.6 %copy-done = bf16[1,4096,256]{2,1,0:T(8,128)(2,1)S(1)} copy-done((bf16[1,4096,256]{2,1,0:T(8,128)(2,1)S(1)}, bf16[1,4096,256]{2,1,0:T(8,128)(2,1)}, u32[]{:S(2)}) %copy-start) | copy-done | bytes 2097176
  2.2 0.0 copy-start.1
  2.2 0.8 copy-done.1
  3.0 0.0 copy-start.2
  3.0 0.7 copy-done.2
  3.7 93.5 %shard_map.50 = (bf16[4096,256]{1,0:T(8,128)(2,1)S(1)}, f32[1]{0:T(128)}) custom-call(bf16[1,3,4096]{2,1,0:T(4,128)(2,1)S(1)} %copy-done.1, s32[6,128]{1,0:T(8,128)S(1)} %bitcast.5, bf16[4096,256]{1,0:T(8,128)(2,1)S(1)} %bitcast.4), custom_call_target="tpu_custom_call" | custom-call | flops 3221225472 | bytes 4194304 | tf_op jit(solution)/shard_map/pallas_call | solution.py:368
  97.1 1.3 %copy.7 = bf16[1,4096,256]{2,1,0:T(8,128)(2,1)} copy(bf16[1,4096,256]{2,1,0:T(8,128)(2,1)S(1)} %bitcast.3) | data formatting | bytes 4194304
Async XLA Ops:
  0.6 1.6 %copy-start = (bf16[1,4096,256]{2,1,0:T(8,128)(2,1)S(1)}, bf16[1,4096,256]{2,1,0:T(8,128)(2,1)}, u32[]{:S(2)}) copy-start(bf16[1,4096,256]{2,1,0:T(8,128)(2,1)} %param.4) | copy-start | bytes 6291460
  2.2 0.8 copy-start.1
  3.0 0.7 copy-start.2

commit v2 on v1

v2 whole, which is shorter than its diff:
```python
import jax
import jax.numpy as jnp
from jax import lax
from jax.experimental import pallas as pl
from jax.experimental.pallas import tpu as pltpu
from jax.sharding import Mesh
from jax.sharding import PartitionSpec as P

Z, Y, X, C = 16, 2, 4, 2
PEERS = Y * X * C
D = 4096
COLS = 256
ROWS = 3
PLANE = PEERS * ROWS
TOKENS = Z * PLANE
UNIT = D // PEERS
HALF = PEERS // 2
CHUNKS = 4
STEPS = Z // 2
LAG = 3
LANES = 128
GROUPS = TOKENS // LANES
TINY = 1e-37
DISTILL = 0.5
VMEM_BYTES = 63 * 1024 * 1024

MESH = pl.DeviceIdType.MESH
F32 = jnp.float32
BF16 = jnp.bfloat16


def arrived(ref, sem):
    pltpu.make_async_copy(ref, ref, sem).wait()


def send(src, dst, send_sem, recv_sem, **where):
    pltpu.make_async_remote_copy(
        src_ref=src,
        dst_ref=dst,
        send_sem=send_sem,
        recv_sem=recv_sem,
        device_id=where,
        device_id_type=MESH,
    ).start()


def plane_peer(j):
    return {"y": j // (X * C), "x": lax.rem(j // C, X), "c": lax.rem(j, C)}


def kernel(
    hidden_hbm, targets_hbm, weight_hbm, grad_hbm, loss_ref,
    own_rows, targets, weight, hbuf, pad, abuf, logits, ebuf, pbuf, gt, tcol, mcol, lcol, tsum,
    lrow, mrow, plrow, pmrow, s1, prow, s2, trow, ptrow, kmsg, k1, zmsg, z1, obuf,
    wsem, hsem, tsem, asem, zsem_a, zsem_b, bsem, ysem, xsem, csem, esem, ssem, osem, out_sems,
):
    z, y, x, c = (lax.axis_index(n) for n in ("z", "y", "x", "c"))
    copy = lax.axis_index("copy")
    me = (y * X + x) * C + c
    unit = c * HALF + x * Y + y

    load_rows = pltpu.make_async_copy(hidden_hbm.at[0], own_rows, hsem)
    load_rows.start()

    def back(t):
        return lax.rem(z - t + Z, Z)

    def ahead(t):
        return lax.rem(z + t, Z)

    right, left = ahead(1), back(1)
    barrier = pltpu.get_barrier_semaphore()

    def meet(**where):
        pl.semaphore_signal(barrier, inc=1, device_id=where, device_id_type=MESH)

    def greet(k, carry):
        meet(**plane_peer(lax.rem(me + k, PEERS)))
        return carry

    meet(z=right)
    meet(z=left)
    meet(copy=1 - copy)
    lax.fori_loop(1, PEERS, greet, 0)

    load_targets = pltpu.make_async_copy(targets_hbm, targets, tsem)
    load_targets.start()
    load_weight = pltpu.make_async_copy(weight_hbm, weight, wsem)
    load_weight.start()

    pad[...] = jnp.zeros_like(pad)
    load_rows.wait()
    own = own_rows[...].astype(F32)
    for q in range(PEERS):
        pad[q, 0:ROWS, :] = own[:, q * UNIT : (q + 1) * UNIT]

    pl.semaphore_wait(barrier, PEERS + 2)

    def unit_of(j):
        return lax.rem(j, C) * HALF + lax.rem(j // C, X) * Y + j // (X * C)

    def scatter(k, carry):
        j = lax.rem(me + k, PEERS)
        send(pad.at[unit_of(j)], abuf.at[me], out_sems.at[0], asem, **plane_peer(j))
        return carry

    lax.fori_loop(1, PEERS, scatter, 0)
    abuf[pl.ds(me, 1)] = pad[pl.ds(unit, 1)]

    row = lax.broadcasted_iota(jnp.int32, (PLANE, PEERS * 8), 0)
    col = lax.broadcasted_iota(jnp.int32, (PLANE, PEERS * 8), 1)
    pick = (row == ROWS * (col >> 3) + (col & 7)) & ((col & 7) < ROWS)
    pick = jnp.where(pick, 1.0, 0.0).astype(BF16)

    eye = lax.broadcasted_iota(jnp.int32, (LANES, LANES), 0) == lax.broadcasted_iota(
        jnp.int32, (LANES, LANES), 1
    )

    def to_row(column):
        return jnp.sum(jnp.where(eye, column, 0.0), axis=0, keepdims=True)

    def to_column(row):
        return jnp.sum(jnp.where(eye, row, 0.0), axis=1, keepdims=True)

    def group(b):
        return slice(b * LANES, (b + 1) * LANES)

    load_targets.wait()
    for b in range(GROUPS):
        tcol[group(b), :] = to_column(targets[b : b + 1, :].astype(F32)).astype(jnp.int32)
    tsum[...] = jnp.zeros_like(tsum)
    offset = ((z * Y + y) * (X * C) + x * C + c) * COLS

    arrived(abuf.at[pl.ds(0, PEERS - 1)], asem)
    block = abuf[...].reshape(PEERS * 8, UNIT).astype(BF16)
    hbuf[z, unit] = jnp.dot(pick, block, preferred_element_type=F32).astype(BF16)

    def at(p, first, count):
        return hbuf.at[p, pl.ds(first, count)]

    def move(ref, sem_out, sem_in, **where):
        send(ref, ref, out_sems.at[sem_out], sem_in, **where)

    def onward(direction):
        return right if direction == 0 else left

    def for_planes(t, do):
        @pl.when((t >= 0) & (t <= STEPS))
        def _():
            do(back(t))

        @pl.when((t >= 1) & (t <= STEPS - 1))
        def _():
            do(ahead(t))

    def a_enter(p, t, direction):
        ref = at(p, unit, 1)

        @pl.when(t > 0)
        def _():
            arrived(ref, zsem_a.at[direction, t])

        @pl.when(t < STEPS - direction)
        def _():
            move(ref, 1, zsem_a.at[direction, t + 1], z=onward(direction))

    def a_first(p):
        move(at(p, unit, 1), 2, ysem.at[p], y=1 - y)

    def a_second(p):
        arrived(at(p, unit, 1), ysem.at[p])
        ref = at(p, x * Y, Y)
        for k in range(1, X):
            move(ref, 3, xsem.at[k - 1, p], x=lax.rem(x + k, X))

    def a_third(p):
        for k in range(1, X):
            arrived(at(p, lax.rem(x + X - k, X) * Y, Y), xsem.at[k - 1, p])
        move(at(p, 0, HALF), 4, csem.at[p], c=1 - c)

    def a_step(i):
        @pl.when(i <= STEPS)
        def _():
            a_enter(back(i), i, 0)

        @pl.when(i <= STEPS - 1)
        def _():
            a_enter(ahead(i), i, 1)

        for_planes(i, a_first)
        for_planes(i - 1, a_second)
        for_planes(i - 2, a_third)

    def b_spread(k, carry):
        j = lax.rem(me // C + k, HALF)
        move(at(z, unit, 1), 5, bsem, y=j // X, x=lax.rem(j, X))
        return carry

    def b_enter(p, t, direction, k):
        size = HALF // CHUNKS
        ref = at(p, HALF + k * size, size)

        @pl.when(t > 0)
        def _():
            arrived(ref, zsem_b.at[direction, t, k])

        @pl.when(t < STEPS - direction)
        def _():
            move(ref, 6, zsem_b.at[direction, t + 1, k], z=onward(direction))

    def b_share(p):
        move(at(p, HALF, HALF), 4, csem.at[p], c=1 - c)

    def b_step(i):
        for k in range(CHUNKS):
            @pl.when(i <= STEPS)
            def _():
                b_enter(back(i), i, 0, k)

            @pl.when(i <= STEPS - 1)
            def _():
                b_enter(ahead(i), i, 1, k)

        for_planes(i, b_share)

    @pl.when(c == 1)
    def _():
        lax.fori_loop(1, HALF, b_spread, 0)
        arrived(hbuf.at[z, pl.ds(HALF, HALF - 1)], bsem)

    load_weight.wait()

    def compute(u):
        planes = (back(u), ahead(u - 1))
        for p in planes:
            arrived(at(p, (1 - c) * HALF, HALF), csem.at[p])
        acc = jnp.zeros((2 * PLANE, COLS), F32)
        for q in range(PEERS):
            both = jnp.concatenate([hbuf[p, q] for p in planes], axis=0)
            acc += jnp.dot(both, weight[q * UNIT : (q + 1) * UNIT, :], preferred_element_type=F32)
        top = jnp.max(acc, axis=1, keepdims=True)
        e = jnp.exp(acc - top)
        lse = top + jnp.log(jnp.sum(e, axis=1, keepdims=True))
        ids = offset + lax.broadcasted_iota(jnp.int32, (PLANE, COLS), 1)
        for k, p in enumerate(planes):
            mine = slice(k * PLANE, (k + 1) * PLANE)
            rows = pl.ds(pl.multiple_of(p * PLANE, PLANE), PLANE)
            logits[rows, :] = acc[mine]
            mcol[rows, :] = top[mine]
            lcol[rows, :] = lse[mine]
            ebuf[rows, :] = e[mine].astype(BF16)
            send(ebuf.at[rows, :], pbuf.at[rows, :], out_sems.at[7], esem, copy=1 - copy)
            hit = jnp.where(ids == tcol[rows, :], acc[mine], 0.0)
            tsum[...] += jnp.sum(hit.reshape(PLANE // 8, 8, COLS), axis=0)

    def step(i, carry):
        @pl.when(c == 0)
        def _():
            a_step(i)

        @pl.when(c == 1)
        def _():
            b_step(i)

        @pl.when(i > LAG)
        def _():
            compute(i - LAG)

        return carry

    lax.fori_loop(0, STEPS + LAG + 1, step, 0)

    def to_plane(src, dst, sem_out, sem_in):
        def one(k, carry):
            send(src, dst.at[me], out_sems.at[sem_out], sem_in, **plane_peer(lax.rem(me + k, PEERS)))
            return carry

        lax.fori_loop(1, PEERS, one, 0)
        dst[pl.ds(me, 1)] = src[...][None]

    def to_line(src, dst, sem_out, sem_in):
        def one(k, carry):
            send(src, dst.at[z], out_sems.at[sem_out], sem_in, z=lax.rem(z + k, Z))
            return carry

        lax.fori_loop(1, Z, one, 0)
        dst[pl.ds(z, 1)] = src[...][None]

    def merged(parts):
        top = jnp.max(parts, axis=0)
        return top + jnp.log(jnp.sum(jnp.exp(parts - top[None]), axis=0))

    for b in range(GROUPS):
        lrow[b : b + 1, :] = to_row(lcol[group(b), :])
    to_plane(lrow, s1, 8, ssem.at[0])
    send(lrow, plrow, out_sems.at[9], ssem.at[1], copy=1 - copy)
    for b in range(GROUPS):
        mrow[b : b + 1, :] = to_row(mcol[group(b), :])
    send(mrow, pmrow, out_sems.at[10], ssem.at[2], copy=1 - copy)
    arrived(s1.at[pl.ds(0, PEERS - 1)], ssem.at[0])
    prow[...] = merged(s1[...])
    to_line(prow, s2, 11, ssem.at[3])

    arrived(plrow, ssem.at[1])
    arrived(pmrow, ssem.at[2])
    arrived(pbuf, esem)
    kmsg[...] = jnp.zeros_like(kmsg)
    for b in range(GROUPS):
        other = pbuf[group(b), :].astype(F32)
        apart = jnp.log(jnp.maximum(other, TINY)) - logits[group(b), :]
        weighted = jnp.sum(other * apart, axis=1, keepdims=True)
        mean = to_row(weighted / jnp.sum(other, axis=1, keepdims=True))
        kmsg[b : b + 1, :] = mean + pmrow[b : b + 1, :]
        kmsg[8 + b : 9 + b, :] = plrow[b : b + 1, :]
    hits = jnp.sum(tsum[...], axis=0, keepdims=True)
    kmsg[GROUPS : GROUPS + 1, :] = hits[:, :LANES] + hits[:, LANES:]
    to_plane(kmsg, k1, 12, ssem.at[4])

    arrived(s2.at[pl.ds(0, Z - 1)], ssem.at[3])
    trow[...] = merged(s2[...])
    send(trow, ptrow, out_sems.at[13], ssem.at[5], copy=1 - copy)

    total = trow[...]
    ids = offset + lax.broadcasted_iota(jnp.int32, (LANES, COLS), 1)
    for b in range(GROUPS):
        probs = jnp.exp(logits[group(b), :] - to_column(total[b : b + 1, :]))
        hot = jnp.where(ids == tcol[group(b), :], 1.0, 0.0)
        logits[group(b), :] = (1.0 + DISTILL) * probs - hot
    arrived(k1.at[pl.ds(0, PEERS - 1)], ssem.at[4])
    plane_kl = k1[:, 0:GROUPS, :]
    plane_lse = k1[:, 8 : 8 + GROUPS, :]
    plane_hits = jnp.sum(k1[:, GROUPS : GROUPS + 1, :], axis=0)

    arrived(ptrow, ssem.at[5])
    partner_total = ptrow[...]
    kl = jnp.sum(jnp.exp(plane_lse - partner_total[None]) * plane_kl, axis=0)
    zmsg[...] = DISTILL * jnp.sum(kl, axis=0, keepdims=True) - plane_hits
    to_line(zmsg, z1, 14, ssem.at[6])

    scale = DISTILL * jnp.exp(pmrow[...] - partner_total)
    for b in range(GROUPS):
        other = pbuf[group(b), :].astype(F32) * to_column(scale[b : b + 1, :])
        gt[:, group(b)] = (logits[group(b), :] - other).astype(BF16).T

    for q in range(PEERS):
        block = hbuf[:, q].reshape(TOKENS, UNIT)
        flipped = jnp.dot(gt[...], block, preferred_element_type=F32)
        obuf[q] = flipped.astype(BF16).T
        pltpu.make_async_copy(obuf.at[q], grad_hbm.at[pl.ds(q * UNIT, UNIT), :], osem).start()

    arrived(z1.at[pl.ds(0, Z - 1)], ssem.at[6])
    per_token = (1.0 + DISTILL) * total - DISTILL * partner_total
    loss_ref[0] = (jnp.sum(z1[...]) + jnp.sum(per_token)) * (1.0 / TOKENS)

    units = hbuf.at[0]
    arrived(pad.at[pl.ds(0, PEERS - 1)], out_sems.at[0])
    arrived(hbuf.at[pl.ds(0, HALF)], out_sems.at[4])

    @pl.when(c == 0)
    def _():
        arrived(units.at[pl.ds(0, Z - 1)], out_sems.at[1])
        arrived(units, out_sems.at[2])
        arrived(hbuf.at[pl.ds(0, 2 * (X - 1))], out_sems.at[3])

    @pl.when(c == 1)
    def _():
        arrived(units.at[pl.ds(0, HALF - 1)], out_sems.at[5])
        arrived(hbuf.at[pl.ds(0, Z - 1), pl.ds(0, HALF)], out_sems.at[6])

    arrived(ebuf, out_sems.at[7])
    arrived(s1.at[pl.ds(0, PEERS - 1)], out_sems.at[8])
    arrived(lrow, out_sems.at[9])
    arrived(mrow, out_sems.at[10])
    arrived(s2.at[pl.ds(0, Z - 1)], out_sems.at[11])
    arrived(k1.at[pl.ds(0, PEERS - 1)], out_sems.at[12])
    arrived(trow, out_sems.at[13])
    arrived(z1.at[pl.ds(0, Z - 1)], out_sems.at[14])
    arrived(obuf, osem)


def body(hidden, head_weight, targets):
    dma = pltpu.SemaphoreType.DMA
    stat = pltpu.VMEM((GROUPS, LANES), F32)
    hbm = pl.BlockSpec(memory_space=pltpu.HBM)
    grad, loss = pl.pallas_call(
        kernel,
        out_shape=(
            jax.ShapeDtypeStruct((D, COLS), BF16),
            jax.ShapeDtypeStruct((1,), F32),
        ),
        in_specs=[hbm, hbm, hbm],
        out_specs=(
            hbm,
            pl.BlockSpec(memory_space=pltpu.SMEM),
        ),
        scratch_shapes=[
            pltpu.VMEM((ROWS, D), BF16),
            pltpu.VMEM((GROUPS, LANES), jnp.int32),
            pltpu.VMEM((D, COLS), BF16),
            pltpu.VMEM((Z, PEERS, PLANE, UNIT), BF16),
            pltpu.VMEM((PEERS, 8, UNIT), F32),
            pltpu.VMEM((PEERS, 8, UNIT), F32),
            pltpu.VMEM((TOKENS, COLS), F32),
            pltpu.VMEM((TOKENS, COLS), BF16),
            pltpu.VMEM((TOKENS, COLS), BF16),
            pltpu.VMEM((COLS, TOKENS), BF16),
            pltpu.VMEM((TOKENS, 1), jnp.int32),
            pltpu.VMEM((TOKENS, 1), F32),
            pltpu.VMEM((TOKENS, 1), F32),
            pltpu.VMEM((8, COLS), F32),
            stat,
            stat,
            stat,
            stat,
            pltpu.VMEM((PEERS, GROUPS, LANES), F32),
            stat,
            pltpu.VMEM((Z, GROUPS, LANES), F32),
            stat,
            stat,
            pltpu.VMEM((16, LANES), F32),
            pltpu.VMEM((PEERS, 16, LANES), F32),
            pltpu.VMEM((1, LANES), F32),
            pltpu.VMEM((Z, 1, LANES), F32),
            pltpu.VMEM((PEERS, UNIT, COLS), BF16),
            dma,
            dma,
            dma,
            dma,
            dma((2, STEPS + 1)),
            dma((2, STEPS + 1, CHUNKS)),
            dma,
            dma((Z,)),
            dma((X - 1, Z)),
            dma((Z,)),
            dma,
            dma((7,)),
            dma,
            dma((15,)),
        ],
        compiler_params=pltpu.CompilerParams(
            collective_id=0, has_side_effects=True, vmem_limit_bytes=VMEM_BYTES
        ),
        cost_estimate=pl.CostEstimate(
            flops=4 * TOKENS * D * COLS,
            bytes_accessed=4 * D * COLS,
            transcendentals=3 * TOKENS * COLS,
        ),
    )(hidden, targets.reshape(GROUPS, LANES), head_weight[0])
    return grad[None], loss


def solution(mesh):
    torus = Mesh(
        mesh.devices.reshape(mesh.shape["copy"], Z, Y, X, C), ("copy", "z", "y", "x", "c")
    )
    everywhere = ("z", "y", "x", "c")
    in_specs = (P("copy", everywhere, None), P("copy", None, everywhere), P())
    out_specs = (P("copy", None, everywhere), P("copy"))
    return jax.shard_map(body, mesh=torus, in_specs=in_specs, out_specs=out_specs, check_vma=False)
```

time: 101 us -> 83 us (0.82)
  Pallas kernels: 93.5 us -> 77 us
  local copies, waits for them, and re-layouts: 4.35 us -> 3.05 us
    pallas_call x1, Pallas kernels: 93.5 us -> 77 us  [body(): pl.pallas_call(kernel, out_shape=(jax.ShapeDtypeStruct((D, COLS), BF16),...]
    unnamed x7 -> x1, local copies, waits for them, and re-layouts: 4.35 us -> 3.05 us
where the time goes in v2:
time: 83 us; the launch traced here: 82.5 us
  Pallas kernels  77 us (93%)
  local copies, waits for them, and re-layouts  3.05 us (4%)
  between operations  2.37 us (3%)
    pallas_call x1, Pallas kernels, body(): pl.pallas_call(kernel, out_shape=(jax.ShapeDtypeStruct((D, COLS), BF16),...  77 us
    unnamed x1, local copies, waits for them, and re-layouts  3.05 us

profile of v2, /device:TPU:1, one launch (start us, length us, event | category | flops | bytes accessed | tf_op | source)
XLA Modules:
  0.0 82.5 jit_solution(16776743061568510704)
XLA Ops:
  0.6 77.0 %shard_map.50 = (bf16[4096,256]{1,0:T(8,128)(2,1)}, f32[1]{0:T(128)}) custom-call(bf16[1,3,4096]{2,1,0:T(4,128)(2,1)} %hidden_hbm.1, s32[6,128]{1,0:T(8,128)} %bitcast.5, bf16[4096,256]{1,0:T(8,128)(2,1)} %bitcast.4), custom_call_target="tpu_custom_call" | custom-call | flops 3221225472 | bytes 4194304 | tf_op jit(solution)/shard_map/pallas_call | solution.py:385
  77.7 3.0 %copy.7 = bf16[1,4096,256]{2,1,0:T(8,128)(2,1)} copy(bf16[1,4096,256]{2,1,0:T(8,128)(2,1)} %bitcast.3) | data formatting | bytes 4194304

commit v3 on v2

v3 whole, which is shorter than its diff:
```python
import jax
import jax.numpy as jnp
from jax import lax
from jax.experimental import pallas as pl
from jax.experimental.pallas import tpu as pltpu
from jax.sharding import Mesh
from jax.sharding import PartitionSpec as P

Z, Y, X, C = 16, 2, 4, 2
PEERS = Y * X * C
D = 4096
COLS = 256
ROWS = 3
PLANE = PEERS * ROWS
TOKENS = Z * PLANE
CHIPS = X * Y
UNIT = 256
SPLIT = CHIPS * UNIT
SUBS = 2 * CHIPS
CHUNKS = 4
STEPS = Z // 2
LAG = 4
LANES = 128
GROUPS = TOKENS // LANES
TINY = 1e-37
DISTILL = 0.5
VMEM_BYTES = 63 * 1024 * 1024

ARRIVE = ((0, 1), (15, 2), (4, 12), (8, 3), (13, 5), (11, 14), (6, 10), (7, 9))
WORK = ((0, 1), (15, 2), (4, 12), (3, 13), (5, 11), (14, 6), (10, 7), (9, 8))

MESH = pl.DeviceIdType.MESH
F32 = jnp.float32
BF16 = jnp.bfloat16


def arrived(ref, sem):
    pltpu.make_async_copy(ref, ref, sem).wait()


def send(src, dst, send_sem, recv_sem, **where):
    pltpu.make_async_remote_copy(
        src_ref=src,
        dst_ref=dst,
        send_sem=send_sem,
        recv_sem=recv_sem,
        device_id=where,
        device_id_type=MESH,
    ).start()


def plane_peer(j):
    return {"y": j // (X * C), "x": lax.rem(j // C, X), "c": lax.rem(j, C)}


def kernel(
    hidden_hbm, targets_hbm, weight_hbm, grad_hbm, loss_ref,
    own_rows, targets, weight, ha, hb, stage_a, stage_b, pad_a, pad_b, abuf_a, abuf_b, logits, ebuf, pbuf, gt, tcol, mcol, lcol, tsum,
    lrow, mrow, plrow, pmrow, s1, prow, s2, trow, ptrow, kmsg, k1, krow, zmsg, z1, lossv, l1, obuf,
    wsem, hsem, tsem, asem, zsem_a, zsem_b, ysem, xsem, csem, esem, ssem, osem, near, out_sems,
):
    z, y, x, c = (lax.axis_index(n) for n in ("z", "y", "x", "c"))
    copy = lax.axis_index("copy")
    me = (y * X + x) * C + c
    unit = x * Y + y

    load_rows = pltpu.make_async_copy(hidden_hbm.at[0], own_rows, hsem)
    load_rows.start()

    def back(t):
        return lax.rem(z - t + Z, Z)

    def ahead(t):
        return lax.rem(z + t, Z)

    right, left = ahead(1), back(1)
    barrier = pltpu.get_barrier_semaphore()

    def meet(**where):
        pl.semaphore_signal(barrier, inc=1, device_id=where, device_id_type=MESH)

    def greet(k, carry):
        meet(**plane_peer(lax.rem(me + k, PEERS)))
        return carry

    meet(z=right)
    meet(z=left)
    meet(copy=1 - copy)
    lax.fori_loop(1, PEERS, greet, 0)

    load_targets = pltpu.make_async_copy(targets_hbm, targets, tsem)
    load_targets.start()
    load_weight = pltpu.make_async_copy(weight_hbm, weight, wsem)
    load_weight.start()

    stage_a[...] = jnp.zeros_like(stage_a)
    load_rows.wait()
    own = own_rows[...].astype(F32)
    for s in range(SUBS):
        for r in range(ROWS):
            half = own[r : r + 1, s * LANES : (s + 1) * LANES]
            stage_a[s // 2, 2 * r + s % 2 : 2 * r + s % 2 + 1, :] = half
            half = own[r : r + 1, SPLIT + s * LANES : SPLIT + (s + 1) * LANES]
            stage_b[s : s + 1, r * LANES : (r + 1) * LANES] = half
    pad_a[...] = stage_a[...].astype(BF16)
    pad_b[...] = stage_b[...].astype(BF16)

    pl.semaphore_wait(barrier, PEERS + 2)

    def give_first(y_to, x_to):
        send(
            pad_a.at[x_to * Y + y_to], abuf_a.at[me], out_sems.at[0], asem, y=y_to, x=x_to, c=0
        )

    def give_last(y_to, x_to):
        send(pad_b, abuf_b.at[me], out_sems.at[15], asem, y=y_to, x=x_to, c=1)

    def scatter(k, carry):
        chip = lax.rem(me // C + k, CHIPS)
        give_last(chip // X, lax.rem(chip, X))
        give_first(chip // X, lax.rem(chip, X))
        return carry

    lax.fori_loop(1, CHIPS, scatter, 0)

    @pl.when(c == 0)
    def _():
        give_last(y, x)
        abuf_a[pl.ds(me, 1)] = pad_a[pl.ds(unit, 1)]

    @pl.when(c == 1)
    def _():
        give_first(y, x)
        abuf_b[pl.ds(me, 1)] = pad_b[...][None]

    eye = lax.broadcasted_iota(jnp.int32, (LANES, LANES), 0) == lax.broadcasted_iota(
        jnp.int32, (LANES, LANES), 1
    )

    def to_row(column):
        return jnp.sum(jnp.where(eye, column, 0.0), axis=0, keepdims=True)

    def to_column(row):
        return jnp.sum(jnp.where(eye, row, 0.0), axis=1, keepdims=True)

    def group(b):
        return slice(b * LANES, (b + 1) * LANES)

    def selector(height, source):
        row = lax.broadcasted_iota(jnp.int32, (height, PEERS * 16), 0)
        col = lax.broadcasted_iota(jnp.int32, (1, PEERS * 16), 1)
        return jnp.where(row == source(col >> 4, col & 15), 1.0, 0.0).astype(BF16)

    def pick(chosen, block):
        return jnp.dot(chosen, block, preferred_element_type=F32)

    def move(ref, sem_out, sem_in, **where):
        send(ref, ref, out_sems.at[sem_out], sem_in, **where)

    def entry(table, t, k):
        digits = sum(pair[k] << (4 * n) for n, pair in enumerate(table[:7]))
        return jnp.where(t == 7, table[7][k], (digits >> (4 * jnp.minimum(t, 6))) & 15)

    def a_onward(p):
        for to in (right, left, ahead(2)):
            move(ha.at[p, unit], 1, zsem_a.at[p], z=to)

    def a_enter(p, further, opposite=False):
        ref = ha.at[p, unit]

        @pl.when(p != z)
        def _():
            arrived(ref, zsem_a.at[p])

        @pl.when(further)
        def _():
            a_onward(p)

        @pl.when(opposite)
        def _():
            move(ref, 1, zsem_a.at[p], z=ahead(4))

        move(ref, 2, ysem.at[p], y=1 - y)

    def a_second(p):
        arrived(ha.at[p, unit], ysem.at[p])
        ref = ha.at[p, pl.ds(x * Y, Y)]
        for k in range(1, X):
            move(ref, 3, xsem.at[k - 1, p], x=lax.rem(x + k, X))

    def a_third(p):
        for k in range(1, X):
            arrived(ha.at[p, pl.ds(lax.rem(x + X - k, X) * Y, Y)], xsem.at[k - 1, p])
        move(ha.at[p], 4, csem.at[p], c=1 - c)

    def a_step(i):
        @pl.when(i < STEPS)
        def _():
            a_enter(back(entry(ARRIVE, i, 0)), (i == 2) | (i == 3), i == 2)
            a_enter(back(entry(ARRIVE, i, 1)), i == 2)

        for lag, do in ((1, a_second), (3, a_third)):
            @pl.when((i >= lag) & (i < STEPS + lag))
            def _():
                for k in range(2):
                    do(back(entry(ARRIVE, i - lag, k)))

    @pl.when(c == 0)
    def _():
        for distance in (1, 2):
            for p in (ahead(distance), back(distance)):
                pl.semaphore_signal(
                    near.at[distance - 1], inc=1, device_id={"z": p}, device_id_type=MESH
                )
            pl.semaphore_wait(near.at[distance - 1], 2)
        chosen = []
        for h in range(2):
            def source(j, at, h=h):
                used = (at < 2 * ROWS) & ((at & 1) == h)
                return jnp.where(used, ROWS * j + (at >> 1), -1)

            chosen.append(selector(PLANE, source))
        arrived(abuf_a.at[pl.ds(0, PEERS - 1)], asem)
        block = abuf_a[...].reshape(PEERS * 16, LANES)
        halves = [pick(one, block) for one in chosen]
        ha[z, unit] = jnp.concatenate(halves, axis=1).astype(BF16)
        for p in (ahead(4), back(4)):
            move(ha.at[z, unit], 1, zsem_a.at[z], z=p)
        a_onward(z)

    def b_enter(p, t, direction, k):
        size = CHIPS // CHUNKS
        ref = hb.at[p, pl.ds(k * size, size)]

        @pl.when(t > 0)
        def _():
            arrived(ref, zsem_b.at[direction, t, k])

        @pl.when(t < STEPS - direction)
        def _():
            move(ref, 6, zsem_b.at[direction, t + 1, k], z=right if direction == 0 else left)

    def b_share(p):
        move(hb.at[p], 5, csem.at[p], c=1 - c)

    def b_step(i):
        for k in range(CHUNKS):
            @pl.when(i <= STEPS)
            def _():
                b_enter(back(i), i, 0, k)

            @pl.when(i < STEPS)
            def _():
                b_enter(ahead(i), i, 1, k)

        @pl.when(i <= STEPS)
        def _():
            b_share(back(i))

        @pl.when((i >= 1) & (i < STEPS))
        def _():
            b_share(ahead(i))

    @pl.when(c == 1)
    def _():
        chosen = [
            selector(SUBS * PLANE, lambda j, s, r=r: s * PLANE + ROWS * j + r) for r in range(ROWS)
        ]
        arrived(abuf_b.at[pl.ds(0, PEERS - 1)], asem)
        block = abuf_b[...].reshape(PEERS * 16, ROWS * LANES)
        plane = sum(
            pick(one, block[:, r * LANES : (r + 1) * LANES]) for r, one in enumerate(chosen)
        )
        plane = plane.astype(BF16)
        for s in range(SUBS):
            half = slice(s % 2 * LANES, (s % 2 + 1) * LANES)
            hb[z, s // 2, :, half] = plane[s * PLANE : (s + 1) * PLANE]
        b_step(0)

    load_targets.wait()
    for b in range(GROUPS):
        tcol[group(b), :] = to_column(targets[b : b + 1, :].astype(F32)).astype(jnp.int32)
    tsum[...] = jnp.zeros_like(tsum)
    offset = ((z * Y + y) * (X * C) + x * C + c) * COLS
    load_weight.wait()

    def spans(load):
        for ref, start in ((ha, 0), (hb, SPLIT)):
            for k in range(2):
                parts = [load(ref, q) for q in range(k * 4, (k + 1) * 4)]
                yield jnp.concatenate(parts, axis=1), start + k * 4 * UNIT, 4 * UNIT

    def compute(u):
        planes = [back(entry(WORK, u, k)) for k in range(2)]
        for p in planes:
            @pl.when(c == 0)
            def _():
                arrived(hb.at[p], csem.at[p])

            @pl.when(c == 1)
            def _():
                arrived(ha.at[p], csem.at[p])

        acc = jnp.zeros((2 * PLANE, COLS), F32)
        for parts, first, width in spans(lambda ref, q: jnp.concatenate([ref[p, q] for p in planes], axis=0)):
            acc += jnp.dot(parts, weight[first : first + width, :], preferred_element_type=F32)
        top = jnp.max(acc, axis=1, keepdims=True)
        e = jnp.exp(acc - top)
        lse = top + jnp.log(jnp.sum(e, axis=1, keepdims=True))
        ids = offset + lax.broadcasted_iota(jnp.int32, (PLANE, COLS), 1)
        for k, p in enumerate(planes):
            mine = slice(k * PLANE, (k + 1) * PLANE)
            rows = pl.ds(pl.multiple_of(p * PLANE, PLANE), PLANE)
            logits[rows, :] = acc[mine]
            mcol[rows, :] = top[mine]
            lcol[rows, :] = lse[mine]
            ebuf[rows, :] = e[mine].astype(BF16)
            send(ebuf.at[rows, :], pbuf.at[rows, :], out_sems.at[7], esem, copy=1 - copy)
            hit = jnp.where(ids == tcol[rows, :], acc[mine], 0.0)
            tsum[...] += jnp.sum(hit.reshape(PLANE // 8, 8, COLS), axis=0)

    def step(i, carry):
        @pl.when(c == 0)
        def _():
            a_step(i)

        @pl.when((c == 1) & (i > 0))
        def _():
            b_step(i)

        u = i - LAG + c

        @pl.when((u >= 0) & (u < STEPS))
        def _():
            compute(u)

        return carry

    lax.fori_loop(0, STEPS + LAG, step, 0)

    def to_plane(src, dst, sem_out, sem_in):
        def one(k, carry):
            send(src, dst.at[me], out_sems.at[sem_out], sem_in, **plane_peer(lax.rem(me + k, PEERS)))
            return carry

        lax.fori_loop(1, PEERS, one, 0)
        dst[pl.ds(me, 1)] = src[...][None]

    def to_line(src, dst, sem_out, sem_in):
        def one(k, carry):
            send(src, dst.at[z], out_sems.at[sem_out], sem_in, z=lax.rem(z + k, Z))
            return carry

        lax.fori_loop(1, Z, one, 0)
        dst[pl.ds(z, 1)] = src[...][None]

    def merged(parts):
        top = jnp.max(parts, axis=0)
        return top + jnp.log(jnp.sum(jnp.exp(parts - top[None]), axis=0))

    for b in range(GROUPS):
        lrow[b : b + 1, :] = to_row(lcol[group(b), :])
    to_plane(lrow, s1, 8, ssem.at[0])
    send(lrow, plrow, out_sems.at[9], ssem.at[1], copy=1 - copy)
    for b in range(GROUPS):
        mrow[b : b + 1, :] = to_row(mcol[group(b), :])
    send(mrow, pmrow, out_sems.at[10], ssem.at[2], copy=1 - copy)
    arrived(s1.at[pl.ds(0, PEERS - 1)], ssem.at[0])
    prow[...] = merged(s1[...])
    to_line(prow, s2, 11, ssem.at[3])

    arrived(plrow, ssem.at[1])
    arrived(pmrow, ssem.at[2])
    arrived(pbuf, esem)
    kmsg[...] = jnp.zeros_like(kmsg)
    for b in range(GROUPS):
        other = pbuf[group(b), :].astype(F32)
        apart = jnp.log(jnp.maximum(other, TINY)) - logits[group(b), :]
        weighted = jnp.sum(other * apart, axis=1, keepdims=True)
        mean = to_row(weighted / jnp.sum(other, axis=1, keepdims=True))
        kmsg[b : b + 1, :] = mean + pmrow[b : b + 1, :]
        kmsg[8 + b : 9 + b, :] = plrow[b : b + 1, :]
    hits = jnp.sum(tsum[...], axis=0, keepdims=True)
    kmsg[GROUPS : GROUPS + 1, :] = hits[:, :LANES] + hits[:, LANES:]
    to_plane(kmsg, k1, 12, ssem.at[4])

    arrived(k1.at[pl.ds(0, PEERS - 1)], ssem.at[4])
    plane_lse = k1[:, 8 : 8 + GROUPS, :]
    plrow_plane = merged(plane_lse)
    krow[...] = jnp.sum(jnp.exp(plane_lse - plrow_plane[None]) * k1[:, 0:GROUPS, :], axis=0)
    plrow[...] = plrow_plane
    line = lax.rem(me, GROUPS)
    zmsg[0:1, :] = plrow[pl.ds(line, 1), :]
    zmsg[1:2, :] = krow[pl.ds(line, 1), :]
    zmsg[2:3, :] = jnp.sum(k1[:, GROUPS : GROUPS + 1, :], axis=0)
    zmsg[3:4, :] = jnp.zeros((1, LANES), F32)
    to_line(zmsg, z1, 14, ssem.at[6])

    arrived(s2.at[pl.ds(0, Z - 1)], ssem.at[3])
    trow[...] = merged(s2[...])
    send(trow, ptrow, out_sems.at[13], ssem.at[5], copy=1 - copy)

    total = trow[...]
    ids = offset + lax.broadcasted_iota(jnp.int32, (LANES, COLS), 1)
    for b in range(GROUPS):
        probs = jnp.exp(logits[group(b), :] - to_column(total[b : b + 1, :]))
        hot = jnp.where(ids == tcol[group(b), :], 1.0, 0.0)
        logits[group(b), :] = (1.0 + DISTILL) * probs - hot
    arrived(z1.at[pl.ds(0, Z - 1)], ssem.at[6])
    line_lse = z1[:, 0:1, :]
    line_kl = z1[:, 1:2, :]
    lossv[...] = DISTILL * jnp.sum(jnp.exp(line_lse - merged(line_lse)[None]) * line_kl, axis=0)
    to_plane(lossv, l1, 16, ssem.at[7])

    arrived(ptrow, ssem.at[5])
    partner_total = ptrow[...]
    scale = DISTILL * jnp.exp(pmrow[...] - partner_total)
    for b in range(GROUPS):
        other = pbuf[group(b), :].astype(F32) * to_column(scale[b : b + 1, :])
        gt[:, group(b)] = (logits[group(b), :] - other).astype(BF16).T

    for block, first, width in spans(lambda ref, q: ref[:, q].reshape(TOKENS, -1)):
        rows = pl.ds(first, width)
        flipped = jnp.dot(gt[...], block, preferred_element_type=F32)
        obuf[rows, :] = flipped.astype(BF16).T
        pltpu.make_async_copy(obuf.at[rows, :], grad_hbm.at[rows, :], osem).start()

    arrived(l1.at[pl.ds(0, PEERS - 1)], ssem.at[7])
    per_token = (1.0 + DISTILL) * total - DISTILL * partner_total
    loss = jnp.sum(per_token) + jnp.sum(l1[0:GROUPS]) - jnp.sum(z1[:, 2:3, :])
    loss_ref[0] = loss * (1.0 / TOKENS)

    @pl.when(c == 0)
    def _():
        arrived(pad_a.at[pl.ds(0, CHIPS - 1)], out_sems.at[0])
        arrived(abuf_b.at[pl.ds(0, CHIPS)], out_sems.at[15])
        arrived(ha.at[pl.ds(0, Z - 1), 0], out_sems.at[1])
        arrived(ha.at[pl.ds(0, Z), 0], out_sems.at[2])
        arrived(ha.at[pl.ds(0, Z), pl.ds(0, Y * (X - 1))], out_sems.at[3])
        arrived(ha, out_sems.at[4])

    @pl.when(c == 1)
    def _():
        arrived(pad_a, out_sems.at[0])
        arrived(abuf_b.at[pl.ds(0, CHIPS - 1)], out_sems.at[15])
        arrived(hb, out_sems.at[5])
        arrived(hb.at[pl.ds(0, Z - 1)], out_sems.at[6])

    arrived(ebuf, out_sems.at[7])
    arrived(s1.at[pl.ds(0, PEERS - 1)], out_sems.at[8])
    arrived(lrow, out_sems.at[9])
    arrived(mrow, out_sems.at[10])
    arrived(s2.at[pl.ds(0, Z - 1)], out_sems.at[11])
    arrived(k1.at[pl.ds(0, PEERS - 1)], out_sems.at[12])
    arrived(trow, out_sems.at[13])
    arrived(z1.at[pl.ds(0, Z - 1)], out_sems.at[14])
    arrived(l1.at[pl.ds(0, PEERS - 1)], out_sems.at[16])
    arrived(obuf, osem)


def body(hidden, head_weight, targets):
    dma = pltpu.SemaphoreType.DMA
    stat = pltpu.VMEM((GROUPS, LANES), F32)
    hbm = pl.BlockSpec(memory_space=pltpu.HBM)
    grad, loss = pl.pallas_call(
        kernel,
        out_shape=(
            jax.ShapeDtypeStruct((D, COLS), BF16),
            jax.ShapeDtypeStruct((1,), F32),
        ),
        in_specs=[hbm, hbm, hbm],
        out_specs=(
            hbm,
            pl.BlockSpec(memory_space=pltpu.SMEM),
        ),
        scratch_shapes=[
            pltpu.VMEM((ROWS, D), BF16),
            pltpu.VMEM((GROUPS, LANES), jnp.int32),
            pltpu.VMEM((D, COLS), BF16),
            pltpu.VMEM((Z, CHIPS, PLANE, UNIT), BF16),
            pltpu.VMEM((Z, CHIPS, PLANE, UNIT), BF16),
            pltpu.VMEM((CHIPS, 16, LANES), F32),
            pltpu.VMEM((16, ROWS * LANES), F32),
            pltpu.VMEM((CHIPS, 16, LANES), BF16),
            pltpu.VMEM((16, ROWS * LANES), BF16),
            pltpu.VMEM((PEERS, 16, LANES), BF16),
            pltpu.VMEM((PEERS, 16, ROWS * LANES), BF16),
            pltpu.VMEM((TOKENS, COLS), F32),
            pltpu.VMEM((TOKENS, COLS), BF16),
            pltpu.VMEM((TOKENS, COLS), BF16),
            pltpu.VMEM((COLS, TOKENS), BF16),
            pltpu.VMEM((TOKENS, 1), jnp.int32),
            pltpu.VMEM((TOKENS, 1), F32),
            pltpu.VMEM((TOKENS, 1), F32),
            pltpu.VMEM((8, COLS), F32),
            stat,
            stat,
            stat,
            stat,
            pltpu.VMEM((PEERS, GROUPS, LANES), F32),
            stat,
            pltpu.VMEM((Z, GROUPS, LANES), F32),
            stat,
            stat,
            pltpu.VMEM((16, LANES), F32),
            pltpu.VMEM((PEERS, 16, LANES), F32),
            stat,
            pltpu.VMEM((4, LANES), F32),
            pltpu.VMEM((Z, 4, LANES), F32),
            pltpu.VMEM((1, LANES), F32),
            pltpu.VMEM((PEERS, 1, LANES), F32),
            pltpu.VMEM((D, COLS), BF16),
            dma,
            dma,
            dma,
            dma,
            dma((Z,)),
            dma((2, STEPS + 1, CHUNKS)),
            dma((Z,)),
            dma((X - 1, Z)),
            dma((Z,)),
            dma,
            dma((8,)),
            dma,
            pltpu.SemaphoreType.REGULAR((2,)),
            dma((17,)),
        ],
        compiler_params=pltpu.CompilerParams(
            collective_id=0, has_side_effects=True, vmem_limit_bytes=VMEM_BYTES
        ),
        cost_estimate=pl.CostEstimate(
            flops=4 * TOKENS * D * COLS,
            bytes_accessed=4 * D * COLS,
            transcendentals=3 * TOKENS * COLS,
        ),
    )(hidden, targets.reshape(GROUPS, LANES), head_weight[0])
    return grad[None], loss


def solution(mesh):
    torus = Mesh(
        mesh.devices.reshape(mesh.shape["copy"], Z, Y, X, C), ("copy", "z", "y", "x", "c")
    )
    everywhere = ("z", "y", "x", "c")
    in_specs = (P("copy", everywhere, None), P("copy", None, everywhere), P())
    out_specs = (P("copy", None, everywhere), P("copy"))
    return jax.shard_map(body, mesh=torus, in_specs=in_specs, out_specs=out_specs, check_vma=False)
```

time: 83 us -> 79.1 us (0.953)
  Pallas kernels: 77 us -> 73.5 us
    pallas_call x1, Pallas kernels: 77 us -> 73.5 us  [body(): pl.pallas_call(kernel, out_shape=(jax.ShapeDtypeStruct((D, COLS), BF16),...]
where the time goes in v3:
time: 79.1 us; the launch traced here: 78.9 us
  Pallas kernels  73.5 us (93%)
  local copies, waits for them, and re-layouts  3.05 us (4%)
  between operations  2.37 us (3%)
    pallas_call x1, Pallas kernels, body(): pl.pallas_call(kernel, out_shape=(jax.ShapeDtypeStruct((D, COLS), BF16),...  73.5 us
    unnamed x1, local copies, waits for them, and re-layouts  3.05 us

profile of v3, /device:TPU:1, one launch (start us, length us, event | category | flops | bytes accessed | tf_op | source)
XLA Modules:
  0.0 78.9 jit_solution(9601807668886521656)
XLA Ops:
  0.6 73.5 %shard_map.50 = (bf16[4096,256]{1,0:T(8,128)(2,1)}, f32[1]{0:T(128)}) custom-call(bf16[1,3,4096]{2,1,0:T(4,128)(2,1)} %hidden_hbm.1, s32[6,128]{1,0:T(8,128)} %bitcast.5, bf16[4096,256]{1,0:T(8,128)(2,1)} %bitcast.4), custom_call_target="tpu_custom_call" | custom-call | flops 3221225472 | bytes 4194304 | tf_op jit(solution)/shard_map/pallas_call | solution.py:465
  74.1 3.0 %copy.7 = bf16[1,4096,256]{2,1,0:T(8,128)(2,1)} copy(bf16[1,4096,256]{2,1,0:T(8,128)(2,1)} %bitcast.3) | data formatting | bytes 4194304

commit v4 on v3

--- a/solution.py
+++ b/solution.py
@@ -19,14 +19,14 @@
 SUBS = 2 * CHIPS
 CHUNKS = 4
 STEPS = Z // 2
-LAG = 4
+LAG = 3
+WAIT = 3
 LANES = 128
 GROUPS = TOKENS // LANES
 TINY = 1e-37
 DISTILL = 0.5
-VMEM_BYTES = 63 * 1024 * 1024
-
-ARRIVE = ((0, 1), (15, 2), (4, 12), (8, 3), (13, 5), (11, 14), (6, 10), (7, 9))
+VMEM_BYTES = 51 * 1024 * 1024
+
 WORK = ((0, 1), (15, 2), (4, 12), (3, 13), (5, 11), (14, 6), (10, 7), (9, 8))
 
 MESH = pl.DeviceIdType.MESH
@@ -55,7 +55,7 @@
 
 def kernel(
     hidden_hbm, targets_hbm, weight_hbm, grad_hbm, loss_ref,
-    own_rows, targets, weight, ha, hb, stage_a, stage_b, pad_a, pad_b, abuf_a, abuf_b, logits, ebuf, pbuf, gt, tcol, mcol, lcol, tsum,
+    own_rows, targets, weight, ha, hb, stage_a, stage_b, pad_a, pad_b, abuf_a, abuf_b, logits, ebuf, pbuf, gt, tcol, mcol, lcol, kcol, tsum,
     lrow, mrow, plrow, pmrow, s1, prow, s2, trow, ptrow, kmsg, k1, krow, zmsg, z1, lossv, l1, obuf,
     wsem, hsem, tsem, asem, zsem_a, zsem_b, ysem, xsem, csem, esem, ssem, osem, near, out_sems,
 ):
@@ -165,10 +165,10 @@
         for to in (right, left, ahead(2)):
             move(ha.at[p, unit], 1, zsem_a.at[p], z=to)
 
-    def a_enter(p, further, opposite=False):
+    def a_enter(p, further, opposite=False, known=False):
         ref = ha.at[p, unit]
 
-        @pl.when(p != z)
+        @pl.when((p != z) & jnp.logical_not(known))
         def _():
             arrived(ref, zsem_a.at[p])
 
@@ -196,14 +196,19 @@
     def a_step(i):
         @pl.when(i < STEPS)
         def _():
-            a_enter(back(entry(ARRIVE, i, 0)), (i == 2) | (i == 3), i == 2)
-            a_enter(back(entry(ARRIVE, i, 1)), i == 2)
+            a_enter(back(entry(WORK, i, 0)), i == 2, i == 2)
+            a_enter(back(entry(WORK, i, 1)), i == 2, known=i == STEPS - 1)
+
+        @pl.when(i == 3)
+        def _():
+            arrived(ha.at[back(8), unit], zsem_a.at[back(8)])
+            a_onward(back(8))
 
         for lag, do in ((1, a_second), (3, a_third)):
             @pl.when((i >= lag) & (i < STEPS + lag))
             def _():
                 for k in range(2):
-                    do(back(entry(ARRIVE, i - lag, k)))
+                    do(back(entry(WORK, i - lag, k)))
 
     @pl.when(c == 0)
     def _():
@@ -212,7 +217,8 @@
                 pl.semaphore_signal(
                     near.at[distance - 1], inc=1, device_id={"z": p}, device_id_type=MESH
                 )
-            pl.semaphore_wait(near.at[distance - 1], 2)
+            if distance == 1:
+                pl.semaphore_wait(near.at[0], 2)
         chosen = []
         for h in range(2):
             def source(j, at, h=h):
@@ -224,9 +230,11 @@
         block = abuf_a[...].reshape(PEERS * 16, LANES)
         halves = [pick(one, block) for one in chosen]
         ha[z, unit] = jnp.concatenate(halves, axis=1).astype(BF16)
-        for p in (ahead(4), back(4)):
+        for p in (right, left):
             move(ha.at[z, unit], 1, zsem_a.at[z], z=p)
-        a_onward(z)
+        pl.semaphore_wait(near.at[1], 2)
+        for p in (ahead(4), back(4), ahead(2)):
+            move(ha.at[z, unit], 1, zsem_a.at[z], z=p)
 
     def b_enter(p, t, direction, k):
         size = CHIPS // CHUNKS
@@ -315,10 +323,20 @@
             mcol[rows, :] = top[mine]
             lcol[rows, :] = lse[mine]
             ebuf[rows, :] = e[mine].astype(BF16)
-            send(ebuf.at[rows, :], pbuf.at[rows, :], out_sems.at[7], esem, copy=1 - copy)
+            send(ebuf.at[rows, :], pbuf.at[rows, :], out_sems.at[7], esem.at[p], copy=1 - copy)
             hit = jnp.where(ids == tcol[rows, :], acc[mine], 0.0)
             tsum[...] += jnp.sum(hit.reshape(PLANE // 8, 8, COLS), axis=0)
 
+    def compare(u):
+        for k in range(2):
+            p = back(entry(WORK, u, k))
+            rows = pl.ds(pl.multiple_of(p * PLANE, PLANE), PLANE)
+            arrived(pbuf.at[rows, :], esem.at[p])
+            other = pbuf[rows, :].astype(F32)
+            apart = jnp.log(jnp.maximum(other, TINY)) - logits[rows, :]
+            weighted = jnp.sum(other * apart, axis=1, keepdims=True)
+            kcol[rows, :] = weighted / jnp.sum(other, axis=1, keepdims=True)
+
     def step(i, carry):
         @pl.when(c == 0)
         def _():
@@ -328,11 +346,15 @@
         def _():
             b_step(i)
 
-        u = i - LAG + c
+        u = i - LAG
 
         @pl.when((u >= 0) & (u < STEPS))
         def _():
             compute(u)
+
+        @pl.when(u >= WAIT)
+        def _():
+            compare(u - WAIT)
 
         return carry
 
@@ -371,14 +393,11 @@
 
     arrived(plrow, ssem.at[1])
     arrived(pmrow, ssem.at[2])
-    arrived(pbuf, esem)
+    for u in range(STEPS - WAIT, STEPS):
+        compare(u)
     kmsg[...] = jnp.zeros_like(kmsg)
     for b in range(GROUPS):
-        other = pbuf[group(b), :].astype(F32)
-        apart = jnp.log(jnp.maximum(other, TINY)) - logits[group(b), :]
-        weighted = jnp.sum(other * apart, axis=1, keepdims=True)
-        mean = to_row(weighted / jnp.sum(other, axis=1, keepdims=True))
-        kmsg[b : b + 1, :] = mean + pmrow[b : b + 1, :]
+        kmsg[b : b + 1, :] = to_row(kcol[group(b), :]) + pmrow[b : b + 1, :]
         kmsg[8 + b : 9 + b, :] = plrow[b : b + 1, :]
     hits = jnp.sum(tsum[...], axis=0, keepdims=True)
     kmsg[GROUPS : GROUPS + 1, :] = hits[:, :LANES] + hits[:, LANES:]
@@ -492,6 +511,7 @@
             pltpu.VMEM((TOKENS, 1), jnp.int32),
             pltpu.VMEM((TOKENS, 1), F32),
             pltpu.VMEM((TOKENS, 1), F32),
+            pltpu.VMEM((TOKENS, 1), F32),
             pltpu.VMEM((8, COLS), F32),
             stat,
             stat,
@@ -519,7 +539,7 @@
             dma((Z,)),
             dma((X - 1, Z)),
             dma((Z,)),
-            dma,
+            dma((Z,)),
             dma((8,)),
             dma,
             pltpu.SemaphoreType.REGULAR((2,)),

time: 79.1 us -> 78.6 us (level)
    unnamed x1 -> x5, local copies, waits for them, and re-layouts: 3.05 us -> 2.76 us
where the time goes in v4:
time: 78.6 us; the launch traced here: 78.3 us
  Pallas kernels  73.2 us (93%)
  local copies, waits for them, and re-layouts  2.76 us (4%)
  between operations  2.41 us (3%)
    pallas_call x1, Pallas kernels, body(): pl.pallas_call(kernel, out_shape=(jax.ShapeDtypeStruct((D, COLS), BF16),...  73.2 us
    unnamed x5, local copies, waits for them, and re-layouts  2.76 us

profile of v4, /device:TPU:1, one launch (start us, length us, event | category | flops | bytes accessed | tf_op | source)
XLA Modules:
  0.0 78.3 jit_solution(13970843851131516038)
XLA Ops:
  0.6 0.0 copy-start
  0.6 0.7 copy-done
  1.4 0.0 copy-start.1
  1.4 0.7 copy-done.1
  2.1 73.2 %shard_map.50 = (bf16[4096,256]{1,0:T(8,128)(2,1)S(1)}, f32[1]{0:T(128)}) custom-call(bf16[1,3,4096]{2,1,0:T(4,128)(2,1)S(1)} %copy-done, s32[6,128]{1,0:T(8,128)S(1)} %bitcast.4, bf16[4096,256]{1,0:T(8,128)(2,1)} %bitcast.5), custom_call_target="tpu_custom_call" | custom-call | flops 3221225472 | bytes 4194304 | tf_op jit(solution)/shard_map/pallas_call | solution.py:484
  75.2 1.3 %copy.7 = bf16[1,4096,256]{2,1,0:T(8,128)(2,1)} copy(bf16[1,4096,256]{2,1,0:T(8,128)(2,1)S(1)} %bitcast.3) | data formatting | bytes 4194304
Async XLA Ops:
  0.6 0.8 copy-start
  1.4 0.7 copy-start.1
